TPU v7x, 32 devices: a whole 2x2x4 slice. The times are simulated.
32 devices in a mesh: expert: 8 (over z, x), replica: 4 (over y, core).
Axes of the slice: x: 2, y: 2, z: 4, core: 2. Of those that a mesh axis runs over, the one named last changes fastest.
Arguments:
- tokens: bfloat16 [8192, 1024], P(('expert', 'replica')), may hold values from -6 to 6
- route: int32 [32, 256], P(('expert', 'replica')), may hold values from 0 to 255, each once within a row
- w_qkv: bfloat16 [1024, 3072], P(('expert', 'replica')), may hold values from -0.1875 to 0.1875
- w_attn_out: bfloat16 [1024, 1024], P(('expert', 'replica')), may hold values from -1 to 1
- w_up: bfloat16 [1024, 4096], P(('expert', 'replica')), may hold values from -0.1875 to 0.1875
- w_down: bfloat16 [4096, 1024], P(('expert', 'replica')), may hold values from -0.09375 to 0.09375
- gain_attn: bfloat16 [1024], P(('expert', 'replica')), may hold values from 0.25 to 1.75
- gain_ffn: bfloat16 [1024], P(('expert', 'replica')), may hold values from 0.25 to 1.75
- expert_in: bfloat16 [8, 1024, 4096], P('expert'), may hold values from -0.1875 to 0.1875
- expert_out: bfloat16 [8, 4096, 1024], P('expert'), may hold values from -0.09375 to 0.09375
- centroids: bfloat16 [8, 1024], P('expert'), may hold values from -0.09375 to 0.09375
- expert_gain: bfloat16 [8, 1024], P('expert'), may hold values from 0.25 to 1.75
- cotangent: bfloat16 [8192, 1024], P(('expert', 'replica')), may hold values from -6 to 6
Outputs:
- mixed: bfloat16 [8192, 1024], P(('expert', 'replica'))
- grad_tokens: float32 [8192, 1024], P(('expert', 'replica'))
- grad_qkv: float32 [1024, 3072], P(('expert', 'replica'))
- grad_attn_out: float32 [1024, 1024], P(('expert', 'replica'))
- grad_up: float32 [1024, 4096], P(('expert', 'replica'))
- grad_down: float32 [4096, 1024], P(('expert', 'replica'))
- grad_gain_attn: float32 [1024], P(('expert', 'replica'))
- grad_gain_ffn: float32 [1024], P(('expert', 'replica'))
- grad_expert_in: float32 [8, 1024, 4096], P('expert', 'replica')
- grad_expert_out: float32 [8, 4096, 1024], P('expert', 'replica')
- grad_centroids: float32 [8, 1024], P('expert', 'replica')
- grad_expert_gain: float32 [8, 1024], P('expert', 'replica')
Inputs may be any that keep to these rules, and one draw needn't show every extreme that they name: `route`: each row is a permutation of 0 to 255.
All inputs are finite; a program needn't handle non-finite values.
Results may differ from a plain program's by a relative error of at most 0.015.
Values may be sent and summed in bfloat16 or wider, within the bound.
No kernel may reach another device: no remote copies, remote signals or barrier semaphores. Data moves between devices by JAX's collectives and lax.ppermute only.
A program may use at most 256 MiB of HBM per device.

v0:
```python
import math

import jax
import jax.numpy as jnp
from jax import lax
from jax.sharding import PartitionSpec as P

HEADS = 16


EPSILON = 1e-05


def layer_norm(values, norm_gain):
    centered = values - jnp.mean(values, axis=-1, keepdims=True)
    inverse = lax.rsqrt(jnp.mean(centered * centered, axis=-1, keepdims=True) + EPSILON)
    normed = centered * inverse
    return (normed * norm_gain, normed, inverse)


def layer_norm_back(grad_out, norm_gain, normed, inverse):
    grad_normed = grad_out * norm_gain
    grad_gain = jnp.sum(grad_out * normed, axis=0)
    grad_in = inverse * (
        grad_normed
        - jnp.mean(grad_normed, axis=-1, keepdims=True)
        - normed * jnp.mean(grad_normed * normed, axis=-1, keepdims=True)
    )
    return (grad_in, grad_gain)


def matmul_rows(left_rows, right_rows):
    return jnp.dot(left_rows, right_rows, preferred_element_type=jnp.float32)


def contract_rows(left_rows, right_rows):
    return lax.dot_general(
        left_rows, right_rows, (((0,), (0,)), ((), ())), preferred_element_type=jnp.float32
    )


def contract_cols(left_rows, right_rows):
    return lax.dot_general(
        left_rows, right_rows, (((1,), (1,)), ((), ())), preferred_element_type=jnp.float32
    )


def group_scores(head_item, causal, factor):
    scores = (
        jnp.einsum(
            "qhd,khd->hqk", head_item[:, 0], head_item[:, 1], preferred_element_type=jnp.float32
        )
        * factor
    )
    return jnp.where(causal, scores, -1e30)


def attend_group(head_item, causal, factor):
    scores = group_scores(head_item, causal, factor)
    largest = jnp.max(scores, axis=-1, keepdims=True)
    shifted = jnp.exp(scores - largest)
    totals = jnp.sum(shifted, axis=-1, keepdims=True)
    weights = (shifted / totals).astype(jnp.bfloat16)
    mixed_heads = jnp.einsum(
        "hqk,khd->qhd", weights, head_item[:, 2], preferred_element_type=jnp.float32
    )
    return (mixed_heads, largest + jnp.log(totals))


def attend_back(head_item, grad_heads, log_total, causal, factor):
    scores = group_scores(head_item, causal, factor)
    probabilities = jnp.exp(scores - log_total)
    weights = probabilities.astype(jnp.bfloat16)
    grad_value = jnp.einsum("hqk,qhd->khd", weights, grad_heads, preferred_element_type=jnp.float32)
    grad_probs = jnp.einsum(
        "qhd,khd->hqk", grad_heads, head_item[:, 2], preferred_element_type=jnp.float32
    )
    row_terms = jnp.sum(grad_probs * probabilities, axis=-1, keepdims=True)
    grad_scores = (probabilities * (grad_probs - row_terms)).astype(jnp.bfloat16)
    grad_query = (
        jnp.einsum("hqk,khd->qhd", grad_scores, head_item[:, 1], preferred_element_type=jnp.float32)
        * factor
    )
    grad_key = (
        jnp.einsum("hqk,qhd->khd", grad_scores, head_item[:, 0], preferred_element_type=jnp.float32)
        * factor
    )
    return jnp.stack([grad_query, grad_key, grad_value], axis=1)


def on_device(
    tokens,
    route,
    w_qkv,
    w_attn_out,
    w_up,
    w_down,
    gain_attn,
    gain_ffn,
    expert_in,
    expert_out,
    centroids,
    expert_gain,
    cotangent,
):
    length, features = tokens.shape
    per_group = min(HEADS, 4)
    groups = HEADS // per_group
    head_size = features // HEADS
    factor = 1.0 / math.sqrt(head_size)
    n_expert = lax.axis_size("expert")
    per_dest = length // n_expert
    full_qkv, full_out, full_up, full_down, full_gain_attn, full_gain_ffn = (
        lax.all_gather(w_qkv, ("expert", "replica"), axis=0, tiled=True),
        lax.all_gather(w_attn_out, ("expert", "replica"), axis=0, tiled=True),
        lax.all_gather(w_up, ("expert", "replica"), axis=0, tiled=True),
        lax.all_gather(w_down, ("expert", "replica"), axis=0, tiled=True),
        lax.all_gather(gain_attn, ("expert", "replica"), axis=0, tiled=True),
        lax.all_gather(gain_ffn, ("expert", "replica"), axis=0, tiled=True),
    )
    gain_one = full_gain_attn.astype(jnp.float32)
    inputs = tokens.astype(jnp.float32)
    attn_in, normed_one, inverse_one = layer_norm(inputs, gain_one)
    attn_in = attn_in.astype(jnp.bfloat16)
    qkv_rows = matmul_rows(attn_in, full_qkv).astype(jnp.bfloat16)
    head_groups = jnp.moveaxis(qkv_rows.reshape(length, 3, groups, per_group, head_size), 2, 0)
    causal = (
        lax.broadcasted_iota(jnp.int32, (length, length), 0)
        >= lax.broadcasted_iota(jnp.int32, (length, length), 1)
    )[None]
    mixed_groups, log_totals = lax.map(
        lambda head_item: attend_group(head_item, causal, factor), head_groups
    )
    heads_out = jnp.moveaxis(mixed_groups, 0, 1).reshape(length, features).astype(jnp.bfloat16)
    hidden = inputs + matmul_rows(heads_out, full_out)
    gain_two = full_gain_ffn.astype(jnp.float32)
    ffn_in, normed_two, inverse_two = layer_norm(hidden, gain_two)
    ffn_in = ffn_in.astype(jnp.bfloat16)
    pre_act = matmul_rows(ffn_in, full_up)
    activated, gelu_back = jax.vjp(jax.nn.gelu, pre_act)
    activated = activated.astype(jnp.bfloat16)
    dense_out = hidden + matmul_rows(activated, full_down)
    route_order = route[0]
    inverse_order = jnp.zeros((length,), jnp.int32).at[route_order].set(lax.iota(jnp.int32, length))
    sent_rows = jnp.take(dense_out.astype(jnp.bfloat16), route_order, axis=0).reshape(
        n_expert, per_dest, features
    )
    arrived = lax.all_to_all(sent_rows, "expert", split_axis=0, concat_axis=0, tiled=True).reshape(
        length, features
    )
    weight_in = expert_in[0]
    weight_out = expert_out[0]
    centroid = centroids[0]
    expert_norm_gain = expert_gain[0].astype(jnp.float32)
    expert_rows = arrived.astype(jnp.float32)
    gate_values = jax.nn.sigmoid(jnp.dot(arrived, centroid, preferred_element_type=jnp.float32))
    expert_norm, normed_three, inverse_three = layer_norm(expert_rows, expert_norm_gain)
    expert_norm = expert_norm.astype(jnp.bfloat16)
    expert_pre = matmul_rows(expert_norm, weight_in)
    expert_act, expert_gelu_back = jax.vjp(jax.nn.gelu, expert_pre)
    expert_act = expert_act.astype(jnp.bfloat16)
    expert_whole = expert_rows + matmul_rows(expert_act, weight_out)
    delta_rows = (gate_values[:, None] * expert_whole).astype(jnp.bfloat16)
    returned = lax.all_to_all(
        delta_rows.reshape(n_expert, per_dest, features),
        "expert",
        split_axis=0,
        concat_axis=0,
        tiled=True,
    ).reshape(length, features)
    mixed = (dense_out + jnp.take(returned, inverse_order, axis=0).astype(jnp.float32)).astype(
        jnp.bfloat16
    )
    grad_sent = jnp.take(cotangent, route_order, axis=0).reshape(n_expert, per_dest, features)
    grad_delta = (
        lax.all_to_all(grad_sent, "expert", split_axis=0, concat_axis=0, tiled=True)
        .reshape(length, features)
        .astype(jnp.float32)
    )
    grad_gate = jnp.sum(grad_delta * expert_whole, axis=-1)
    grad_logit = grad_gate * gate_values * (1.0 - gate_values)
    grad_whole = gate_values[:, None] * grad_delta
    grad_whole_low = grad_whole.astype(jnp.bfloat16)
    grad_weight_out = contract_rows(expert_act, grad_whole_low)
    grad_expert_act = contract_cols(grad_whole_low, weight_out)
    grad_expert_pre = expert_gelu_back(grad_expert_act)[0].astype(jnp.bfloat16)
    grad_weight_in = contract_rows(expert_norm, grad_expert_pre)
    grad_expert_norm = contract_cols(grad_expert_pre, weight_in)
    grad_from_norm, grad_norm_gain = layer_norm_back(
        grad_expert_norm, expert_norm_gain, normed_three, inverse_three
    )
    grad_centroid = jnp.dot(grad_logit, expert_rows, precision=lax.Precision.HIGHEST)
    grad_rows = grad_whole + grad_logit[:, None] * centroid.astype(jnp.float32) + grad_from_norm
    grad_home = lax.all_to_all(
        grad_rows.astype(jnp.bfloat16).reshape(n_expert, per_dest, features),
        "expert",
        split_axis=0,
        concat_axis=0,
        tiled=True,
    ).reshape(length, features)
    sum_expert_in, sum_expert_out, sum_centroids, sum_expert_gain = (
        lax.psum_scatter(
            grad_weight_in[None].astype(jnp.bfloat16), "replica", scatter_dimension=1, tiled=True
        ).astype(jnp.float32),
        lax.psum_scatter(
            grad_weight_out[None].astype(jnp.bfloat16), "replica", scatter_dimension=1, tiled=True
        ).astype(jnp.float32),
        lax.psum_scatter(
            grad_centroid[None].astype(jnp.bfloat16), "replica", scatter_dimension=1, tiled=True
        ).astype(jnp.float32),
        lax.psum_scatter(
            grad_norm_gain[None].astype(jnp.bfloat16), "replica", scatter_dimension=1, tiled=True
        ).astype(jnp.float32),
    )
    grad_dense = cotangent.astype(jnp.float32) + jnp.take(grad_home, inverse_order, axis=0).astype(
        jnp.float32
    )
    grad_dense_low = grad_dense.astype(jnp.bfloat16)
    grad_down = contract_rows(activated, grad_dense_low)
    grad_act = contract_cols(grad_dense_low, full_down)
    grad_pre = gelu_back(grad_act)[0].astype(jnp.bfloat16)
    grad_up = contract_rows(ffn_in, grad_pre)
    grad_ffn_in = contract_cols(grad_pre, full_up)
    grad_hidden_norm, grad_gain_ffn = layer_norm_back(
        grad_ffn_in, gain_two, normed_two, inverse_two
    )
    grad_hidden = grad_dense + grad_hidden_norm
    grad_hidden_low = grad_hidden.astype(jnp.bfloat16)
    grad_attn_out = contract_rows(heads_out, grad_hidden_low)
    grad_heads = contract_cols(grad_hidden_low, full_out).astype(jnp.bfloat16)
    grad_groups = jnp.moveaxis(grad_heads.reshape(length, groups, per_group, head_size), 1, 0)
    grad_qkv_groups = lax.map(
        lambda group_item: attend_back(group_item[0], group_item[1], group_item[2], causal, factor),
        (head_groups, grad_groups, log_totals),
    )
    grad_qkv_rows = (
        jnp.moveaxis(grad_qkv_groups, 0, 2).reshape(length, 3 * features).astype(jnp.bfloat16)
    )
    grad_qkv = contract_rows(attn_in, grad_qkv_rows)
    grad_attn_in = contract_cols(grad_qkv_rows, full_qkv)
    grad_input_norm, grad_gain_attn = layer_norm_back(
        grad_attn_in, gain_one, normed_one, inverse_one
    )
    grad_tokens = grad_hidden + grad_input_norm
    sum_qkv, sum_out, sum_up, sum_down, sum_gain_attn, sum_gain_ffn = (
        lax.psum_scatter(grad_qkv, ("expert", "replica"), scatter_dimension=0, tiled=True),
        lax.psum_scatter(grad_attn_out, ("expert", "replica"), scatter_dimension=0, tiled=True),
        lax.psum_scatter(grad_up, ("expert", "replica"), scatter_dimension=0, tiled=True),
        lax.psum_scatter(grad_down, ("expert", "replica"), scatter_dimension=0, tiled=True),
        lax.psum_scatter(grad_gain_attn, ("expert", "replica"), scatter_dimension=0, tiled=True),
        lax.psum_scatter(grad_gain_ffn, ("expert", "replica"), scatter_dimension=0, tiled=True),
    )
    return (
        mixed,
        grad_tokens,
        sum_qkv,
        sum_out,
        sum_up,
        sum_down,
        sum_gain_attn,
        sum_gain_ffn,
        sum_expert_in,
        sum_expert_out,
        sum_centroids,
        sum_expert_gain,
    )


def solution(mesh):
    placed = (
        P(("expert", "replica"), None),
        P(("expert", "replica"), None),
        P(("expert", "replica"), None),
        P(("expert", "replica"), None),
        P(("expert", "replica"), None),
        P(("expert", "replica"), None),
        P(("expert", "replica")),
        P(("expert", "replica")),
        P("expert", None, None),
        P("expert", None, None),
        P("expert", None),
        P("expert", None),
        P(("expert", "replica"), None),
    )
    return jax.shard_map(
        on_device,
        mesh=mesh,
        in_specs=placed,
        out_specs=(
            P(("expert", "replica"), None),
            P(("expert", "replica"), None),
            P(("expert", "replica"), None),
            P(("expert", "replica"), None),
            P(("expert", "replica"), None),
            P(("expert", "replica"), None),
            P(("expert", "replica")),
            P(("expert", "replica")),
            P("expert", "replica", None),
            P("expert", "replica", None),
            P("expert", "replica"),
            P("expert", "replica"),
        ),
        check_vma=False,
    )
```

profile of v0, /device:TPU:0, one launch (start us, length us, event | category | flops | bytes accessed | tf_op | source)
XLA Modules:
  0.0 1242.1 jit_solution(14710888254416083744)
XLA Ops:
  11.7 42.3 %all-reduce.5 = (bf16[1024]{0:T(1024)(128)(2,1)S(1)}, bf16[1024]{0:T(1024)(128)(2,1)S(1)}) all-reduce(bf16[1024]{0:T(1024)(128)(2,1)S(1)} %dynamic-update-slice, bf16[1024]{0:T(1024)(128)(2,1)S(1)} %dynamic-update-slice.1), channel_id=1, replica_groups=mesh['expert'=8,'replica'=4] {'expert','replica'}, use_global_device_ids=true, to_apply=%add | all-reduce | flops 2048 | bytes 8192
  54.7 3.5 gather_fusion.2
  58.7 24.6 %all-gather.5.cloned.1.call-done = bf16[1024,3072]{1,0:T(8,128)(2,1)} async-done(((bf16[32,3072]{1,0:T(8,128)(2,1)}), bf16[1024,3072]{1,0:T(8,128)(2,1)}) %all-gather.5.cloned.1.call-update) | async-done | bytes 6291472 | tf_op jit(solution)/shard_map/all_gather | solution.py:114
  83.3 4.7 convolution_convert_fusion
  88.0 1.6 copy.44
  89.6 1.6 copy.45
  91.2 3.8 while.24
  95.0 46.1 %all-gather.7.cloned.1.call-done = bf16[1024,1024]{1,0:T(8,128)(2,1)} async-done(((bf16[32,1024]{1,0:T(8,128)(2,1)}), bf16[1024,1024]{1,0:T(8,128)(2,1)}) %all-gather.7.cloned.1.call-update) | async-done | bytes 2097168 | tf_op jit(solution)/shard_map/all_gather | solution.py:115
  141.1 2.6 fusion.109
  144.0 76.4 %all-gather.9.cloned.1.call-done = bf16[1024,4096]{1,0:T(8,128)(2,1)} async-done(((bf16[32,4096]{1,0:T(8,128)(2,1)}), bf16[1024,4096]{1,0:T(8,128)(2,1)}) %all-gather.9.cloned.1.call-update) | async-done | bytes 8388624 | tf_op jit(solution)/shard_map/all_gather | solution.py:116
  220.4 7.8 fusion.107
  228.3 71.1 %all-gather.11.cloned.1.call-done = bf16[4096,1024]{1,0:T(8,128)(2,1)} async-done(((bf16[128,1024]{1,0:T(8,128)(2,1)}), bf16[4096,1024]{1,0:T(8,128)(2,1)}) %all-gather.11.cloned.1.call-update) | async-done | bytes 8388624 | tf_op jit(solution)/shard_map/all_gather | solution.py:117
  299.4 8.4 fusion.110
  310.1 4.0 all-to-all-start
  314.1 14.9 %all-to-all-done = bf16[8,32,1024]{2,1,0:T(8,128)(2,1)S(1)} async-done(((bf16[8,32,1024]{2,1,0:T(8,128)(2,1)}), bf16[8,32,1024]{2,1,0:T(8,128)(2,1)S(1)}, u32[]{:S(2)}, u32[]{:S(2)}) %all-to-all-start) | async-done | bytes 524320 | tf_op jit(solution)/shard_map/all_to_all | solution.py:148
  329.0 3.6 all-to-all-start.2
  334.1 7.8 fusion.31
  341.9 5.5 all-to-all-done.2
  347.4 8.4 fusion.84
  356.0 12.1 fusion.46
  369.5 7.5 fusion.80
  377.9 11.0 reduce-scatter.21.cloned.1.call-start
  388.9 7.4 convert_bitcast_fusion.1
  396.5 3.2 fusion.81
  399.6 5.2 convert_bitcast_fusion
  404.9 18.1 %all_to_all.20 = bf16[8,32,1024]{2,1,0:T(8,128)(2,1)S(1)} all-to-all(bf16[8,32,1024]{2,1,0:T(8,128)(2,1)S(1)} %bitcast.222), channel_id=1, replica_groups=mesh['expert'=8,'replica'=4] {'expert'}, dimensions={0} | all-to-all | bytes 1048576 | tf_op jit(solution)/shard_map/all_to_all | solution.py:194
  422.9 3.6 all-to-all-start.1
  428.1 2.0 gather_fusion.3
  430.0 10.7 all-to-all-done.1
  440.7 2.0 gather_fusion.1
  442.7 9.6 fusion.39
  452.3 6.8 multiply_reduce_fusion.1
  461.6 2.8 fusion.90
  464.7 3.5 convolution_convert_fusion.1
  468.1 2.1 copy.46
  470.2 17.7 %while.25 = (s32[]{:T(128)}, bf16[4,256,3,4,64]{1,4,3,0,2:T(8,128)(2,1)}, bf16[4,256,3,4,64]{1,4,3,2,0:T(8,128)(2,1)S(1)}, f32[4,4,256,1]{2,1,3,0:T(4,128)S(1)}, bf16[4,256,4,64]{1,3,2,0:T(8,128)(2,1)}, /*index=5*/s32[]{:T(128)}) while((s32[]{:T(128)}, bf16[4,256,3,4,64]{1,4,3,0,2:T(8,128)(2,1)}, ...), condition=%wide.region_18.20_spmd.clone, body=%wide.region_16.19_spmd.clone.sunk | while | flops 171637760 | bytes 10899553 | solution.py:232
  487.9 9.9 fusion.103
  497.8 10.4 fusion.106
  509.3 11.2 fusion.97
  523.7 6.0 fusion.64
  529.7 38.0 %all-reduce.4 = (f32[1024]{0:T(1024)S(1)}, f32[1024]{0:T(1024)S(1)}) all-reduce(f32[1024]{0:T(1024)S(1)} %get-tuple-element.120, f32[1024]{0:T(1024)S(1)} %get-tuple-element.116), channel_id=6, replica_groups=mesh['expert'=8,'replica'=4] {'expert','replica'}, use_global_device_ids=true, to_apply=%region_26.28.clone | all-reduce | flops 2048 | bytes 16384
  568.9 2.6 fusion.63
  571.5 4.1 convert_element_type.206
  575.6 4.1 convert_element_type.210
  579.7 124.9 %reduce-scatter.15.cloned.1.call-done = f32[32,1024]{1,0:T(8,128)} async-done(((f32[1024,1024]{1,0:T(8,128)}), f32[32,1024]{1,0:T(8,128)}) %reduce-scatter.15.cloned.1.call-update) | async-done | bytes 131088 | tf_op jit(solution)/shard_map/reduce_scatter | solution.py:247
  704.5 157.7 %reduce-scatter.13.cloned.1.call-done = f32[32,3072]{1,0:T(8,128)} async-done(((f32[1024,3072]{1,0:T(8,128)}), f32[32,3072]{1,0:T(8,128)}) %reduce-scatter.13.cloned.1.call-update) | async-done | bytes 393232 | tf_op jit(solution)/shard_map/reduce_scatter | solution.py:246
  862.3 185.2 %reduce-scatter.17.cloned.1.call-done = f32[32,4096]{1,0:T(8,128)} async-done(((f32[1024,4096]{1,0:T(8,128)}), f32[32,4096]{1,0:T(8,128)}) %reduce-scatter.17.cloned.1.call-update) | async-done | bytes 524304 | tf_op jit(solution)/shard_map/reduce_scatter | solution.py:248
  1047.4 187.4 %reduce-scatter.19.cloned.1.call-done = f32[128,1024]{1,0:T(8,128)} async-done(((f32[4096,1024]{1,0:T(8,128)}), f32[128,1024]{1,0:T(8,128)}) %reduce-scatter.19.cloned.1.call-update) | async-done | bytes 524304 | tf_op jit(solution)/shard_map/reduce_scatter | solution.py:249
  (188 shorter events, 42.9 us)
Async XLA Ops:
  7.2 51.5 %copy-start.18 = (s32[1,256]{1,0:T(1,128)S(1)}, s32[1,256]{1,0:T(1,128)}, u32[]{:S(2)}) copy-start(s32[1,256]{1,0:T(1,128)} %param.20) | copy-start | bytes 3076
  7.2 51.0 %copy-start.5 = (bf16[256,1024]{1,0:T(8,128)(2,1)S(1)}, bf16[256,1024]{1,0:T(8,128)(2,1)}, u32[]{:S(2)}) copy-start(bf16[256,1024]{1,0:T(8,128)(2,1)} %param.19) | copy-start | bytes 1572868
  7.2 76.1 %all-gather.5.cloned.1.call-start = ((), (), s32[]{:S(2)}) async-start(), calls=%async_computation.12 | async-start | bytes 6488064 | tf_op jit(solution)/shard_map/all_gather | solution.py:114
  7.9 133.2 %all-gather.7.cloned.1.call-start = ((), (), s32[]{:S(2)}) async-start(), calls=%async_computation.13 | async-start | bytes 2162688 | tf_op jit(solution)/shard_map/all_gather | solution.py:115
  8.7 211.8 %all-gather.9.cloned.1.call-start = ((), (), s32[]{:S(2)}) async-start(), calls=%async_computation.14 | async-start | bytes 8650752 | tf_op jit(solution)/shard_map/all_gather | solution.py:116
  9.4 289.9 %all-gather.11.cloned.1.call-start = ((), (), s32[]{:S(2)}) async-start(), calls=%async_computation.15 | async-start | bytes 8650752 | tf_op jit(solution)/shard_map/all_gather | solution.py:117
  95.0 46.2 %copy-start.12 = (bf16[4,256,4,64]{1,3,2,0:T(8,128)(2,1)}, bf16[4,256,4,64]{1,3,2,0:T(8,128)(2,1)S(1)}, u32[]{:S(2)}) copy-start(bf16[4,256,4,64]{1,3,2,0:T(8,128)(2,1)S(1)} %get-tuple-element.73) | copy-start | bytes 1572868
  143.7 155.6 %copy-start.1 = (f32[256,1024]{1,0:T(8,128)}, f32[256,1024]{1,0:T(8,128)S(1)}, u32[]{:S(2)}) copy-start(f32[256,1024]{1,0:T(8,128)S(1)} %get-tuple-element.161) | copy-start | bytes 3145732
  307.8 1.2 copy-start.10
  307.8 6.4 copy-start.17
  308.9 25.0 %copy-start.16 = (bf16[1,1024]{1,0:T(2,128)(2,1)S(1)}, bf16[1,1024]{1,0:T(2,128)(2,1)}, u32[]{:S(2)}) copy-start(bf16[1,1024]{1,0:T(2,128)(2,1)} %param.29) | copy-start | bytes 6148
  310.1 19.0 %all-to-all-start = ((bf16[8,32,1024]{2,1,0:T(8,128)(2,1)}), bf16[8,32,1024]{2,1,0:T(8,128)(2,1)S(1)}, u32[]{:S(2)}, u32[]{:S(2)}) async-start(bf16[8,32,1024]{2,1,0:T(8,128)(2,1)} %bitcast.223), calls=%async_computation | async-start | bytes 1048576 | tf_op jit(solution)/shard_map/all_to_all | solution.py:148
  329.0 18.3 %all-to-all-start.2 = ((bf16[8,32,1024]{2,1,0:T(8,128)(2,1)}), bf16[8,32,1024]{2,1,0:T(8,128)(2,1)S(1)}, u32[]{:S(2)}, u32[]{:S(2)}) async-start(bf16[8,32,1024]{2,1,0:T(8,128)(2,1)} %bitcast.221), calls=%async_computation.2 | async-start | bytes 1048576 | tf_op jit(solution)/shard_map/all_to_all | solution.py:176
  332.7 187.8 %reduce-scatter.25.cloned.1.call-start = ((), (), s32[]{:S(2)}) async-start(), calls=%async_computation.22 | async-start | bytes 327680
  369.4 152.8 %reduce-scatter.27.cloned.1.call-start = ((), (), s32[]{:S(2)}) async-start(), calls=%async_computation.23 | async-start | bytes 327680
  377.9 193.5 %reduce-scatter.21.cloned.1.call-start = ((), (), s32[]{:S(2)}) async-start(), calls=%async_computation.20 | async-start | bytes 10485760 | tf_op jit(solution)/shard_map/reduce_scatter | solution.py:202
  396.3 179.2 %reduce-scatter.23.cloned.1.call-start = ((), (), s32[]{:S(2)}) async-start(), calls=%async_computation.21 | async-start | bytes 10485760 | tf_op jit(solution)/shard_map/reduce_scatter | solution.py:205
  396.4 3.2 copy-start.19
  422.9 17.8 %all-to-all-start.1 = ((bf16[8,32,1024]{2,1,0:T(8,128)(2,1)}), bf16[8,32,1024]{2,1,0:T(8,128)(2,1)S(1)}, u32[]{:S(2)}, u32[]{:S(2)}) async-start(bf16[8,32,1024]{2,1,0:T(8,128)(2,1)} %bitcast.14), calls=%async_computation.1 | async-start | bytes 1048576 | tf_op jit(solution)/shard_map/all_to_all | solution.py:164
  426.6 278.0 %reduce-scatter.15.cloned.1.call-start = ((), (), s32[]{:S(2)}) async-start(), calls=%async_computation.17 | async-start | bytes 4325376 | tf_op jit(solution)/shard_map/reduce_scatter | solution.py:247
  428.1 14.6 %copy-start = (bf16[256,1024]{1,0:T(8,128)(2,1)S(1)}, bf16[256,1024]{1,0:T(8,128)(2,1)}, u32[]{:S(2)}) copy-start(bf16[256,1024]{1,0:T(8,128)(2,1)} %param.31) | copy-start | bytes 1572868
  442.7 9.6 copy-start.2
  452.3 6.8 copy-start.9
  452.3 6.9 copy-start.7
  452.3 6.9 copy-start.11
  452.3 6.9 copy-start.15
  459.2 2.4 copy-start.13
  460.6 1.0 copy-start.3
  464.4 397.9 %reduce-scatter.13.cloned.1.call-start = ((), (), s32[]{:S(2)}) async-start(), calls=%async_computation.16 | async-start | bytes 12976128 | tf_op jit(solution)/shard_map/reduce_scatter | solution.py:246
  497.8 549.6 %reduce-scatter.17.cloned.1.call-start = ((), (), s32[]{:S(2)}) async-start(), calls=%async_computation.18 | async-start | bytes 17301504 | tf_op jit(solution)/shard_map/reduce_scatter | solution.py:248
  508.2 1.0 copy-start.8
  508.3 726.6 %reduce-scatter.19.cloned.1.call-start = ((), (), s32[]{:S(2)}) async-start(), calls=%async_computation.19 | async-start | bytes 17301504 | tf_op jit(solution)/shard_map/reduce_scatter | solution.py:249
  520.5 3.2 copy-start.6
  520.5 3.2 copy-start.14
  523.7 45.2 %copy-start.4 = (f32[256,1024]{1,0:T(8,128)S(1)}, f32[256,1024]{1,0:T(8,128)}, u32[]{:S(2)}) copy-start(f32[256,1024]{1,0:T(8,128)} %copy-done.3) | copy-start | bytes 3145732
Sparse Core Ops, SparseCore 0:
  10.9 72.3 all-gather.4
  86.2 54.8 all-gather.6
  144.0 76.4 all-gather.8
  223.2 76.1 all-gather.10
  369.5 18.7 reduce-scatter.24
  390.7 20.0 reduce-scatter.26
  413.4 71.6 reduce-scatter.20
  487.9 72.5 reduce-scatter.22
  563.3 141.1 reduce-scatter.14
  711.0 151.2 reduce-scatter.12
  865.2 182.1 reduce-scatter.16
  1050.2 184.5 reduce-scatter.18
where the time goes:
time: 1250 us; the launch traced here: 1240 us
  waiting for transfers between devices  907 us (73%)
  matrix products  149 us (12%)
  blocking collectives  98.4 us (8%)
  other arithmetic  24.7 us (2%)
  local copies, waits for them, and re-layouts  24.3 us (2%)
  starting transfers between devices  23.2 us (2%)
  between operations  15 us (1%)
    reduce_scatter x1, waiting for transfers between devices, on_device(): lax.psum_scatter(grad_down, ('expert', 'replica'), scatter_dimension=0, t...  187 us
    reduce_scatter x1, waiting for transfers between devices, on_device(): lax.psum_scatter(grad_up, ('expert', 'replica'), scatter_dimension=0, til...  185 us
    reduce_scatter x1, waiting for transfers between devices, on_device(): lax.psum_scatter(grad_qkv, ('expert', 'replica'), scatter_dimension=0, ti...  158 us
    reduce_scatter x1, waiting for transfers between devices, on_device(): lax.psum_scatter(grad_attn_out, ('expert', 'replica'), scatter_dimension=...  125 us
    unnamed x2, blocking collectives  80.4 us
    all_gather x1, waiting for transfers between devices, on_device(): lax.all_gather(w_up, ('expert', 'replica'), axis=0, tiled=True)  76.4 us
    all_gather x1, waiting for transfers between devices, on_device(): lax.all_gather(w_down, ('expert', 'replica'), axis=0, tiled=True)  71.1 us
    dot_general x6, matrix products, contract_rows(): lax.dot_general(left_rows, right_rows, (((0,), (0,)), ((), ())), preferre...  46.8 us
  transfers between devices with their start and end apart: 15, of which 11 were waited for; matrix products, arithmetic and copies ran while one was open for 13% of the time, Pallas kernels for 0%

commit v1 on v0

v1 whole, which is shorter than its diff:
```python
import math

import jax
import jax.numpy as jnp
from jax import lax
from jax.sharding import PartitionSpec as P

HEADS = 16


EPSILON = 1e-05


def layer_norm(values, norm_gain):
    centered = values - jnp.mean(values, axis=-1, keepdims=True)
    inverse = lax.rsqrt(jnp.mean(centered * centered, axis=-1, keepdims=True) + EPSILON)
    normed = centered * inverse
    return (normed * norm_gain, normed, inverse)


def layer_norm_back(grad_out, norm_gain, normed, inverse):
    grad_normed = grad_out * norm_gain
    grad_gain = jnp.sum(grad_out * normed, axis=0)
    grad_in = inverse * (
        grad_normed
        - jnp.mean(grad_normed, axis=-1, keepdims=True)
        - normed * jnp.mean(grad_normed * normed, axis=-1, keepdims=True)
    )
    return (grad_in, grad_gain)


def matmul_rows(left_rows, right_rows):
    return jnp.dot(left_rows, right_rows, preferred_element_type=jnp.float32)


def contract_rows(left_rows, right_rows):
    return lax.dot_general(
        left_rows, right_rows, (((0,), (0,)), ((), ())), preferred_element_type=jnp.float32
    )


def contract_cols(left_rows, right_rows):
    return lax.dot_general(
        left_rows, right_rows, (((1,), (1,)), ((), ())), preferred_element_type=jnp.float32
    )


def group_scores(head_item, causal, factor):
    scores = (
        jnp.einsum(
            "qhd,khd->hqk", head_item[:, 0], head_item[:, 1], preferred_element_type=jnp.float32
        )
        * factor
    )
    return jnp.where(causal, scores, -1e30)


def attend_group(head_item, causal, factor):
    scores = group_scores(head_item, causal, factor)
    largest = jnp.max(scores, axis=-1, keepdims=True)
    shifted = jnp.exp(scores - largest)
    totals = jnp.sum(shifted, axis=-1, keepdims=True)
    weights = (shifted / totals).astype(jnp.bfloat16)
    mixed_heads = jnp.einsum(
        "hqk,khd->qhd", weights, head_item[:, 2], preferred_element_type=jnp.float32
    )
    return (mixed_heads, largest + jnp.log(totals))


def attend_back(head_item, grad_heads, log_total, causal, factor):
    scores = group_scores(head_item, causal, factor)
    probabilities = jnp.exp(scores - log_total)
    weights = probabilities.astype(jnp.bfloat16)
    grad_value = jnp.einsum("hqk,qhd->khd", weights, grad_heads, preferred_element_type=jnp.float32)
    grad_probs = jnp.einsum(
        "qhd,khd->hqk", grad_heads, head_item[:, 2], preferred_element_type=jnp.float32
    )
    row_terms = jnp.sum(grad_probs * probabilities, axis=-1, keepdims=True)
    grad_scores = (probabilities * (grad_probs - row_terms)).astype(jnp.bfloat16)
    grad_query = (
        jnp.einsum("hqk,khd->qhd", grad_scores, head_item[:, 1], preferred_element_type=jnp.float32)
        * factor
    )
    grad_key = (
        jnp.einsum("hqk,qhd->khd", grad_scores, head_item[:, 0], preferred_element_type=jnp.float32)
        * factor
    )
    return jnp.stack([grad_query, grad_key, grad_value], axis=1)

ALL_AXES = ("expert", "replica")


def device_swap(values, bits):
    n_dev = lax.axis_size("expert") * lax.axis_size("replica")
    return lax.ppermute(values, ALL_AXES, [(d, d ^ bits) for d in range(n_dev)])


def swap_core(values):
    return device_swap(values, 1)


def swap_y(values):
    return device_swap(values, 2)


def swap_x(values):
    return device_swap(values, 4)


def plane_shift(values, step):
    n_dev = lax.axis_size("expert") * lax.axis_size("replica")
    return lax.ppermute(values, ALL_AXES, [(d, (d + 8 * step) % n_dev) for d in range(n_dev)])


def after(values, *earlier):
    return lax.optimization_barrier((values,) + earlier)[0]


def rows(*parts):
    return jnp.concatenate(parts, axis=0)


def cols(*parts):
    return jnp.concatenate(parts, axis=1)


def gather_own_core(planes, half):
    stacked = rows(*planes)
    left, right = stacked[:, :half], stacked[:, half:]
    n = left.shape[0]
    left_x = swap_x(left)
    right_y = swap_y(right)
    left_y = swap_y(rows(left, left_x))
    right_x = swap_x(rows(right, right_y))
    return cols(
        rows(left, left_x, left_y), rows(right, right_x[:n], right_y, right_x[n:])
    )


def scatter_sum(total, half, n_planes):
    n = total.shape[0] // 4
    low = total.astype(jnp.bfloat16)
    left, right = low[:, :half], low[:, half:]
    left_f, right_f = total[:, :half], total[:, half:]
    left_y = swap_y(left[2 * n :])
    right_x = swap_x(rows(right[n : 2 * n], right[3 * n :]))
    left_sum = left_f[: 2 * n] + left_y.astype(jnp.float32)
    right_sum = rows(right_f[:n], right_f[2 * n : 3 * n]) + right_x.astype(jnp.float32)
    left_x = swap_x(left_sum[n:].astype(jnp.bfloat16))
    right_y = swap_y(right_sum[n:].astype(jnp.bfloat16))
    both = cols(
        left_sum[:n] + left_x.astype(jnp.float32), right_sum[:n] + right_y.astype(jnp.float32)
    )
    m = n // n_planes
    low_both = both.astype(jnp.bfloat16)
    result = both[:m]
    for step in range(1, n_planes):
        moved = plane_shift(low_both[step * m : (step + 1) * m], step)
        result = result + moved.astype(jnp.float32)
    return result


def on_device(
    tokens,
    route,
    w_qkv,
    w_attn_out,
    w_up,
    w_down,
    gain_attn,
    gain_ffn,
    expert_in,
    expert_out,
    centroids,
    expert_gain,
    cotangent,
):
    length, features = tokens.shape
    per_group = min(HEADS, 4)
    groups = HEADS // per_group
    head_size = features // HEADS
    factor = 1.0 / math.sqrt(head_size)
    n_expert = lax.axis_size("expert")
    n_replica = lax.axis_size("replica")
    n_dev = n_expert * n_replica
    n_planes = n_dev // 8
    per_dest = length // n_expert
    bf16, f32 = jnp.bfloat16, jnp.float32
    replica = lax.axis_index("replica")
    me = lax.axis_index("expert") * n_replica + replica
    rel = lax.iota(jnp.int32, n_dev)
    rel_plane = rel % n_planes
    rel_x = (rel // n_planes) % 2
    rel_y = (rel // (2 * n_planes)) % 2
    rel_core = rel // (4 * n_planes)
    rel_dev = ((me // 8 + rel_plane) % n_planes) * 8 + (
        (me % 8) ^ (4 * rel_x + 2 * rel_y + rel_core)
    )
    shard = features // n_dev
    rel_feature = (rel_dev[:, None] * shard + lax.iota(jnp.int32, shard)[None]).reshape(features)
    to_rel = (lax.iota(jnp.int32, features)[:, None] == rel_feature[None]).astype(bf16)

    padded_gains = jnp.pad(
        jnp.stack([gain_attn, gain_ffn], axis=1), ((0, 0), (0, 126))
    )
    first = cols(w_qkv, w_attn_out, padded_gains)
    width_qkv = w_qkv.shape[1]
    hidden_size = w_up.shape[1]

    def planes_of(own):
        return [own] + [plane_shift(own, n_planes - step) for step in range(1, n_planes)]

    planes_first = planes_of(first)
    planes_up = planes_of(after(w_up, *planes_first[1:]))
    planes_down = planes_of(after(w_down, *planes_up[1:]))
    first_half = gather_own_core(planes_first, 2048)
    first_full = rows(first_half, swap_core(first_half))
    up_half = gather_own_core(planes_up, hidden_size // 2)
    down_half = gather_own_core(planes_down, features // 2)
    full_up = rows(up_half, swap_core(up_half))
    full_down = rows(down_half, swap_core(down_half))
    full_qkv = first_full[:, :width_qkv]
    full_out = first_full[:, width_qkv : width_qkv + features]
    gain_columns = first_full[:, width_qkv + features : width_qkv + features + 2]
    gains_plain = lax.dot_general(
        gain_columns, to_rel, (((0,), (1,)), ((), ())), preferred_element_type=f32
    )
    gains_rel = matmul_rows(gains_plain.astype(bf16), to_rel)
    gain_one = gains_rel[0]
    gain_two = gains_plain[1]
    gain_two_rel = gains_rel[1]

    def rel_order(low_values):
        return matmul_rows(low_values, to_rel).astype(bf16)

    inputs = tokens.astype(f32)
    inputs_rel = rel_order(tokens).astype(f32)
    attn_in, normed_one, inverse_one = layer_norm(inputs_rel, gain_one)
    attn_in = attn_in.astype(bf16)
    qkv_rows = matmul_rows(attn_in, full_qkv).astype(bf16)
    head_groups = jnp.moveaxis(qkv_rows.reshape(length, 3, groups, per_group, head_size), 2, 0)
    causal = (
        lax.broadcasted_iota(jnp.int32, (length, length), 0)
        >= lax.broadcasted_iota(jnp.int32, (length, length), 1)
    )[None]
    mixed_groups, log_totals = lax.map(
        lambda head_item: attend_group(head_item, causal, factor), head_groups
    )
    heads_out = jnp.moveaxis(mixed_groups, 0, 1).reshape(length, features).astype(bf16)
    heads_rel = rel_order(heads_out)
    hidden = inputs + matmul_rows(heads_rel, full_out)
    ffn_in, normed_two, inverse_two = layer_norm(hidden, gain_two)
    ffn_rel = rel_order(ffn_in.astype(bf16))
    pre_act = matmul_rows(ffn_rel, full_up)
    activated, gelu_back = jax.vjp(jax.nn.gelu, pre_act)
    activated = activated.astype(bf16)
    act_rel = jnp.take(activated.reshape(length, n_dev, -1), rel_dev, axis=1).reshape(length, -1)
    dense_out = hidden + matmul_rows(act_rel, full_down)

    route_pick = (route[0][:, None] == lax.iota(jnp.int32, length)[None]).astype(bf16)

    def to_expert(low_values):
        picked = matmul_rows(route_pick, low_values).astype(bf16)
        return lax.all_to_all(
            picked.reshape(n_expert, per_dest, features),
            "expert",
            split_axis=0,
            concat_axis=0,
            tiled=True,
        ).reshape(length, features)

    def to_home(low_values):
        back = lax.all_to_all(
            low_values.reshape(n_expert, per_dest, features),
            "expert",
            split_axis=0,
            concat_axis=0,
            tiled=True,
        ).reshape(length, features)
        return contract_rows(route_pick, back)

    arrived = to_expert(dense_out.astype(bf16))
    weight_in = expert_in[0]
    weight_out = expert_out[0]
    centroid = centroids[0]
    expert_norm_gain = expert_gain[0].astype(f32)
    expert_rows = arrived.astype(f32)
    gate_values = jax.nn.sigmoid(jnp.dot(arrived, centroid, preferred_element_type=f32))
    expert_norm, normed_three, inverse_three = layer_norm(expert_rows, expert_norm_gain)
    expert_norm = expert_norm.astype(bf16)
    expert_pre = matmul_rows(expert_norm, weight_in)
    expert_act, expert_gelu_back = jax.vjp(jax.nn.gelu, expert_pre)
    expert_act = expert_act.astype(bf16)
    expert_whole = expert_rows + matmul_rows(expert_act, weight_out)
    delta_rows = (gate_values[:, None] * expert_whole).astype(bf16)
    mixed = (dense_out + to_home(delta_rows)).astype(bf16)
    grad_delta = to_expert(cotangent).astype(f32)
    grad_gate = jnp.sum(grad_delta * expert_whole, axis=-1)
    grad_logit = grad_gate * gate_values * (1.0 - gate_values)
    grad_whole = gate_values[:, None] * grad_delta
    grad_whole_low = grad_whole.astype(bf16)
    grad_expert_act = contract_cols(grad_whole_low, weight_out)
    grad_expert_pre = expert_gelu_back(grad_expert_act)[0].astype(bf16)
    grad_expert_norm = contract_cols(grad_expert_pre, weight_in)
    grad_from_norm, grad_norm_gain = layer_norm_back(
        grad_expert_norm, expert_norm_gain, normed_three, inverse_three
    )
    grad_centroid = jnp.dot(grad_logit, expert_rows, precision=lax.Precision.HIGHEST)
    grad_rows = grad_whole + grad_logit[:, None] * centroid.astype(f32) + grad_from_norm
    grad_placed = to_home(grad_rows.astype(bf16))

    block = lax.iota(jnp.int32, n_replica)
    copy_order = replica ^ (2 * (block % 2) + block // 2)

    def copies_order(values):
        shape = values.shape[:-1]
        return jnp.take(values.reshape(*shape, n_replica, -1), copy_order, axis=-2).reshape(values.shape)

    def sum_copies(left, right, extra=None):
        left = copies_order(left)
        half = left.shape[1] // 2
        keep, send = contract_rows(left[:, :half], right), contract_rows(left[:, half:], right)
        if extra is not None:
            keep, send = cols(keep, extra[:half]), cols(send, extra[half:])
        total = keep + swap_core(send.astype(bf16)).astype(f32)
        n = half // 2
        return total[:n] + swap_y(total[n:].astype(bf16)).astype(f32)

    sum_expert_out = sum_copies(expert_act, grad_whole_low)
    vectors = jnp.pad(
        copies_order(jnp.stack([grad_centroid, grad_norm_gain])).T, ((0, 0), (0, 126))
    )
    sum_in_all = sum_copies(expert_norm, grad_expert_pre, vectors)
    sum_expert_in = sum_in_all[:, : weight_in.shape[1]]
    sum_vectors = sum_in_all[:, weight_in.shape[1] :]

    def sum_dense(left, right, extra=None):
        half = left.shape[1] // 2
        keep, send = contract_rows(left[:, :half], right), contract_rows(left[:, half:], right)
        if extra is not None:
            keep, send = cols(keep, extra[:half]), cols(send, extra[half:])
        total = keep + swap_core(send.astype(bf16)).astype(f32)
        return scatter_sum(total, right.shape[1] // 2, n_planes)

    grad_dense = cotangent.astype(f32) + grad_placed
    grad_dense_low = grad_dense.astype(bf16)
    sum_down = sum_dense(act_rel, grad_dense_low)
    grad_act_rel = contract_cols(grad_dense_low, full_down)
    plain_order = jnp.zeros((n_dev,), jnp.int32).at[rel_dev].set(lax.iota(jnp.int32, n_dev))
    grad_act = jnp.take(grad_act_rel.reshape(length, n_dev, -1), plain_order, axis=1).reshape(length, -1)
    grad_pre = gelu_back(grad_act)[0].astype(bf16)
    sum_up = sum_dense(ffn_rel, grad_pre)
    grad_ffn_rel = contract_cols(grad_pre, full_up)

    def plain_order_f32(values):
        high = values.astype(bf16)
        low = (values - high.astype(f32)).astype(bf16)
        return contract_cols(high, to_rel) + contract_cols(low, to_rel)

    grad_hidden_norm, grad_gain_ffn = layer_norm_back(
        plain_order_f32(grad_ffn_rel), gain_two, normed_two, inverse_two
    )
    grad_gain_ffn_rel = jnp.dot(grad_gain_ffn, to_rel.astype(f32), precision=lax.Precision.HIGHEST)
    grad_hidden = grad_dense + grad_hidden_norm
    grad_hidden_low = grad_hidden.astype(bf16)
    sum_out = sum_dense(heads_rel, grad_hidden_low)
    grad_heads_rel = contract_cols(grad_hidden_low, full_out).astype(bf16)
    grad_heads = contract_cols(grad_heads_rel, to_rel).astype(bf16)
    grad_groups = jnp.moveaxis(grad_heads.reshape(length, groups, per_group, head_size), 1, 0)
    grad_qkv_groups = lax.map(
        lambda group_item: attend_back(group_item[0], group_item[1], group_item[2], causal, factor),
        (head_groups, grad_groups, log_totals),
    )
    grad_qkv_rows = (
        jnp.moveaxis(grad_qkv_groups, 0, 2).reshape(length, 3 * features).astype(bf16)
    )
    grad_attn_rel = contract_cols(grad_qkv_rows, full_qkv)
    grad_input_norm, grad_gain_attn = layer_norm_back(
        grad_attn_rel, gain_one, normed_one, inverse_one
    )
    grad_tokens = grad_hidden + plain_order_f32(grad_input_norm)
    gain_grads = jnp.pad(jnp.stack([grad_gain_attn, grad_gain_ffn_rel], axis=1), ((0, 0), (0, 126)))
    sum_qkv_all = sum_dense(attn_in, grad_qkv_rows, gain_grads)
    sum_qkv = sum_qkv_all[:, :width_qkv]
    return (
        mixed,
        grad_tokens,
        sum_qkv,
        sum_out,
        sum_up,
        sum_down,
        sum_qkv_all[:, width_qkv],
        sum_qkv_all[:, width_qkv + 1],
        sum_expert_in[None],
        sum_expert_out[None],
        sum_vectors[None, :, 0],
        sum_vectors[None, :, 1],
    )


def solution(mesh):
    placed = (
        P(("expert", "replica"), None),
        P(("expert", "replica"), None),
        P(("expert", "replica"), None),
        P(("expert", "replica"), None),
        P(("expert", "replica"), None),
        P(("expert", "replica"), None),
        P(("expert", "replica")),
        P(("expert", "replica")),
        P("expert", None, None),
        P("expert", None, None),
        P("expert", None),
        P("expert", None),
        P(("expert", "replica"), None),
    )
    return jax.shard_map(
        on_device,
        mesh=mesh,
        in_specs=placed,
        out_specs=(
            P(("expert", "replica"), None),
            P(("expert", "replica"), None),
            P(("expert", "replica"), None),
            P(("expert", "replica"), None),
            P(("expert", "replica"), None),
            P(("expert", "replica"), None),
            P(("expert", "replica")),
            P(("expert", "replica")),
            P("expert", "replica", None),
            P("expert", "replica", None),
            P("expert", "replica"),
            P("expert", "replica"),
        ),
        check_vma=False,
    )
```

time: 1250 us -> 759 us (0.61)
  waiting for transfers between devices: 907 us -> 267 us
  other arithmetic: 24.7 us -> 162 us
  blocking collectives: 98.4 us -> 0 us
  starting transfers between devices: 23.2 us -> 93.6 us
  local copies, waits for them, and re-layouts: 24.3 us -> 82 us
    reduce_scatter x6 -> x0, waiting for transfers between devices: 655 us -> none  [the longest x1 187 us: on_device(): lax.psum_scatter(grad_down, ('expert', 'replica'), scatter_dimension=0, t...]
    ppermute x0 -> x60, waiting for transfers between devices: none -> 251 us  [the longest x39 169 us: device_swap(): return lax.ppermute(values, ALL_AXES, [(d, d ^ bits) for d in range(n_dev)])]
    all_gather x4 -> x0, waiting for transfers between devices: 218 us -> none  [the longest x1 76.4 us: on_device(): lax.all_gather(w_up, ('expert', 'replica'), axis=0, tiled=True)]
    concatenate x0 -> x20, other arithmetic: none -> 99.5 us  [the longest x6 77.8 us: cols(): return jnp.concatenate(parts, axis=1)]
    unnamed x2 -> x0, blocking collectives: 80.4 us -> none
    ppermute x0 -> x60, starting transfers between devices: none -> 73.7 us  [the longest x39 38 us: device_swap(): return lax.ppermute(values, ALL_AXES, [(d, d ^ bits) for d in range(n_dev)])]
    slice x0 -> x37, local copies, waits for them, and re-layouts: none -> 21.6 us  [the longest x2 5.53 us: sum_copies(): return total[:n] + swap_y(total[n:].astype(bf16)).astype(f32)]
    add x1 -> x23, other arithmetic: 2.59 us -> 21.5 us  [the longest x1 9.05 us: sum_copies(): total = keep + swap_core(send.astype(bf16)).astype(f32)]
  transfers between devices with their start and end apart: 15 -> 64, of which waited for: 11 -> 26; matrix products, arithmetic and copies ran while one was open for 13% -> 44% of each run, Pallas kernels for 0% -> 0%
where the time goes in v1:
time: 759 us; the launch traced here: 750 us
  waiting for transfers between devices  267 us (35%)
  other arithmetic  162 us (21%)
  matrix products  142 us (19%)
  starting transfers between devices  93.6 us (12%)
  local copies, waits for them, and re-layouts  82 us (11%)
    ppermute x39, waiting for transfers between devices, device_swap(): return lax.ppermute(values, ALL_AXES, [(d, d ^ bits) for d in range(n_dev)])  169 us
    ppermute x21, waiting for transfers between devices, plane_shift(): lax.ppermute(values, ALL_AXES, [(d, (d + 8 * step) % n_dev) for d in rang...  82 us
    concatenate x6, other arithmetic, cols(): return jnp.concatenate(parts, axis=1)  77.8 us
    dot_general x10, matrix products, contract_cols(): lax.dot_general(left_rows, right_rows, (((1,), (1,)), ((), ())), preferre...  46.9 us
    dot_general x14, matrix products, contract_rows(): lax.dot_general(left_rows, right_rows, (((0,), (0,)), ((), ())), preferre...  38.5 us
    ppermute x39, starting transfers between devices, device_swap(): return lax.ppermute(values, ALL_AXES, [(d, d ^ bits) for d in range(n_dev)])  38 us
    ppermute x21, starting transfers between devices, plane_shift(): lax.ppermute(values, ALL_AXES, [(d, (d + 8 * step) % n_dev) for d in rang...  35.7 us
    dot_general x12, matrix products, matmul_rows(): return jnp.dot(left_rows, right_rows, preferred_element_type=jnp.float32)  33.8 us
  transfers between devices with their start and end apart: 64, of which 26 were waited for; matrix products, arithmetic and copies ran while one was open for 44% of the time, Pallas kernels for 0%

profile of v1, /device:TPU:0, one launch (start us, length us, event | category | flops | bytes accessed | tf_op | source)
XLA Modules:
  0.0 749.8 jit_solution(564001537283450427)
XLA Ops:
  15.1 10.8 %collective-permute-done.1 = bf16[32,4224]{1,0:T(8,128)(2,1)S(1)} collective-permute-done((bf16[32,4224]{1,0:T(8,128)(2,1)S(1)}, bf16[32,4224]{1,0:T(8,128)(2,1)S(1)}, u32[]{:S(2)}, u32[]{:S(2)}) %collective-permute-start.1) | collective-permute-done | bytes 270368 | tf_op jit(solution)/shard_map/ppermute | solution.py:112
  25.9 7.3 collective-permute-start.8
  40.0 16.7 %collective-permute-done.9 = bf16[32,4096]{1,0:T(8,128)(2,1)S(1)} collective-permute-done((bf16[32,4096]{1,0:T(8,128)(2,1)S(1)}, bf16[32,4096]{1,0:T(8,128)(2,1)S(1)}, u32[]{:S(2)}, u32[]{:S(2)}) %collective-permute-start.9) | collective-permute-done | bytes 262176 | tf_op jit(solution)/shard_map/ppermute | solution.py:112
  60.9 22.2 %collective-permute-done.6 = bf16[256,2176]{1,0:T(8,128)(2,1)S(1)} collective-permute-done((bf16[256,2176]{1,0:T(8,128)(2,1)S(1)}, bf16[256,2176]{1,0:T(8,128)(2,1)S(1)}, u32[]{:S(2)}, u32[]{:S(2)}) %collective-permute-start.6) | collective-permute-done | bytes 1114144 | tf_op jit(solution)/shard_map/ppermute | solution.py:95
  83.2 15.3 %maximum_maximum_fusion = bf16[512,4224]{1,0:T(8,128)(2,1)} fusion(bf16[128,2176]{1,0:T(8,128)(2,1)S(1)} %get-tuple-element.182, bf16[128,2176]{1,0:T(8,128)(2,1)S(1)} %collective-permute-done.5, bf16[128,2176]{1,0:T(8,128)(2,1)S(1)} %get-tuple-element.181, bf16[128,2176]{1,0:T(8,128)(2,1)S(1)} %pad_maximum_fusion.19, ...), kind=kLoop, calls=%fused_computation.81 | loop fusion | flops 30277632 | bytes 8650752 | tf_op jit(solution)/shard_map/concatenate | solution.py:124
  106.7 4.9 collective-permute-done.18
  120.1 12.1 %collective-permute-done.21 = bf16[512,512]{1,0:T(8,128)(2,1)S(1)} collective-permute-done((bf16[512,512]{1,0:T(8,128)(2,1)S(1)}, bf16[512,512]{1,0:T(8,128)(2,1)S(1)}, u32[]{:S(2)}, u32[]{:S(2)}) %collective-permute-start.21) | collective-permute-done | bytes 524320 | tf_op jit(solution)/shard_map/ppermute | solution.py:95
  132.8 20.1 %collective-permute-done.19 = bf16[512,512]{1,0:T(8,128)(2,1)S(1)} collective-permute-done((bf16[512,512]{1,0:T(8,128)(2,1)S(1)}, bf16[512,512]{1,0:T(8,128)(2,1)S(1)}, u32[]{:S(2)}, u32[]{:S(2)}) %collective-permute-start.19) | collective-permute-done | bytes 524320 | tf_op jit(solution)/shard_map/ppermute | solution.py:95
  154.7 24.3 %maximum_maximum_fusion.1 = bf16[512,4096]{1,0:T(8,128)(2,1)} fusion(bf16[128,2048]{1,0:T(8,128)(2,1)S(1)} %get-tuple-element.198, bf16[128,2048]{1,0:T(8,128)(2,1)} %collective-permute-done.13, bf16[128,2048]{1,0:T(8,128)(2,1)S(1)} %get-tuple-element.197, bf16[128,2048]{1,0:T(8,128)(2,1)} %get-tuple-element.196, ...), kind=kLoop, calls=%fused_computation.103 | loop fusion | flops 29360128 | bytes 8388608 | tf_op jit(solution)/shard_map/concatenate | solution.py:124
  179.3 31.0 %maximum_maximum_fusion.2 = bf16[2048,1024]{1,0:T(8,128)(2,1)} fusion(bf16[512,512]{1,0:T(8,128)(2,1)S(1)} %get-tuple-element.194, bf16[512,512]{1,0:T(8,128)(2,1)S(1)} %collective-permute-done.21, bf16[512,512]{1,0:T(8,128)(2,1)S(1)} %get-tuple-element.193, bf16[512,512]{1,0:T(8,128)(2,1)S(1)} %get-tuple-element.192, ...), kind=kLoop, calls=%fused_computation.104 | loop fusion | flops 29360128 | bytes 8388608 | tf_op jit(solution)/shard_map/concatenate | solution.py:124
  213.7 7.0 pad_maximum_fusion
  229.1 6.4 while.24
  244.0 5.5 pad_maximum_fusion.1
  258.6 4.1 copy.84
  265.5 6.3 pad_maximum_fusion.2
  277.1 5.5 all-to-all-start
  284.9 12.4 %all-to-all-done = bf16[8,32,1024]{2,1,0:T(8,128)(2,1)S(1)} async-done(((bf16[8,32,1024]{2,1,0:T(8,128)(2,1)}), bf16[8,32,1024]{2,1,0:T(8,128)(2,1)S(1)}, u32[]{:S(2)}, u32[]{:S(2)}) %all-to-all-start) | async-done | bytes 524320 | tf_op jit(solution)/shard_map/all_to_all | solution.py:264
  302.9 9.4 %multiply_convert_fusion.1 = (bf16[256,4096]{1,0:T(8,128)(2,1)}, f32[256,4096]{1,0:T(8,128)}) fusion(bf16[256,1024]{1,0:T(8,128)(2,1)} %bitcast.330, bf16[1,1024,4096]{2,1,0:T(8,128)(2,1)} %param.25), kind=kOutput, calls=%fused_computation.105 | convolution fusion | flops 2156920832 | bytes 15204352 | tf_op jit(solution)/shard_map/dot_general | solution.py:33
  315.6 7.6 %fusion.134 = (f32[256]{0:T(256)S(1)}, f32[256,1024]{1,0:T(8,128)}) fusion(bf16[8,32,1024]{2,1,0:T(8,128)(2,1)S(1)} %all-to-all-done.2, bf16[256,4096]{1,0:T(8,128)(2,1)} %get-tuple-element.212, bf16[1,4096,1024]{2,1,0:T(8,128)(2,1)} %param.26, bf16[256,1024]{1,0:T(8,128)(2,1)S(1)} %bitcast.311), kind=kOutput, calls=%fused_computation.233 | convolution fusion | flops 2148794112 | bytes 12583936 | tf_op jit(solution)/shard_map/dot_general | solution.py:33
  323.5 11.2 %fusion.50 = bf16[256,4096]{1,0:T(8,128)(2,1)S(1)} fusion(f32[256,4096]{1,0:T(8,128)} %get-tuple-element.213, bf16[256,1024]{1,0:T(8,128)(2,1)S(1)} %bitcast.331, bf16[1,4096,1024]{2,1,0:T(8,128)(2,1)} %param.26), kind=kOutput, calls=%fused_computation.96 | convolution fusion | flops 2168455168 | bytes 15204352 | tf_op jit(solution)/shard_map/dot_general | solution.py:43
  334.7 6.8 fusion.120
  343.1 4.5 all-to-all-start.3
  368.4 3.9 copy.97
  378.7 4.6 fusion.159
  383.3 6.2 all-to-all-start.1
  391.1 5.7 convolution_bitcast_fusion.2
  399.4 5.0 gather_fusion.1
  404.4 5.2 fusion.43
  409.6 6.5 fusion.271
  419.9 4.2 fusion.96
  426.2 21.9 %while.25 = (s32[]{:T(128)}, bf16[4,256,3,4,64]{1,4,3,0,2:T(8,128)(2,1)}, bf16[4,256,3,4,64]{1,4,3,2,0:T(8,128)(2,1)}, f32[4,4,256,1]{2,1,3,0:T(4,128)S(1)}, bf16[4,256,4,64]{1,3,2,0:T(8,128)(2,1)}, /*index=5*/s32[]{:T(128)}) while((s32[]{:T(128)}, bf16[4,256,3,4,64]{1,4,3,0,2:T(8,128)(2,1)}, ...), condition=%wide.region_18.19_spmd.clone, body=%wide.region_16.18_spmd.clone.sunk | while | flops 171637760 | bytes 10899553 | solution.py:370
  448.0 6.3 fusion.110
  468.7 3.9 pad_maximum_fusion.4
  483.7 5.6 collective-permute-done.33
  498.1 3.7 collective-permute-start.39
  512.6 7.5 fusion.247
  532.3 9.0 %maximum_add_fusion = f32[512,4224]{1,0:T(8,128)} fusion(f32[512,128]{1,0:T(8,128)S(1)} %copy-done.79, f32[512,4096]{1,0:T(8,128)} %fusion.159, bf16[512,4224]{1,0:T(8,128)(2,1)} %collective-permute-done.56), kind=kLoop, calls=%fused_computation.53 | loop fusion | flops 6488064 | bytes 21626880 | tf_op jit(solution)/shard_map/add | solution.py:325
  541.3 3.9 slice.725
  563.9 33.5 %collective-permute-done.28 = bf16[128,1664]{1,0:T(8,128)(2,1)S(1)} collective-permute-done((bf16[128,1664]{1,0:T(8,128)(2,1)S(1)}, bf16[128,1664]{1,0:T(8,128)(2,1)S(1)}, u32[]{:S(2)}, u32[]{:S(2)}) %collective-permute-start.28) | collective-permute-done | bytes 426016 | tf_op jit(solution)/shard_map/ppermute | solution.py:95
  600.8 4.5 collective-permute-done.31
  606.4 8.9 %collective-permute-done.30 = bf16[32,3200]{1,0:T(8,128)(2,1)S(1)} collective-permute-done((bf16[32,3200]{1,0:T(8,128)(2,1)S(1)}, bf16[32,3200]{1,0:T(8,128)(2,1)S(1)}, u32[]{:S(2)}, u32[]{:S(2)}) %collective-permute-start.30) | collective-permute-done | bytes 204832 | tf_op jit(solution)/shard_map/ppermute | solution.py:112
  623.9 17.5 %collective-permute-done.43 = bf16[256,2048]{1,0:T(8,128)(2,1)S(1)} collective-permute-done((bf16[256,2048]{1,0:T(8,128)(2,1)S(1)}, bf16[256,2048]{1,0:T(8,128)(2,1)S(1)}, u32[]{:S(2)}, u32[]{:S(2)}) %collective-permute-start.43) | collective-permute-done | bytes 1048608 | tf_op jit(solution)/shard_map/ppermute | solution.py:95
  644.0 43.9 %collective-permute-done.49 = bf16[1024,512]{1,0:T(8,128)(2,1)S(1)} collective-permute-done((bf16[1024,512]{1,0:T(8,128)(2,1)S(1)}, bf16[1024,512]{1,0:T(8,128)(2,1)S(1)}, u32[]{:S(2)}, u32[]{:S(2)}) %collective-permute-start.49) | collective-permute-done | bytes 1048608 | tf_op jit(solution)/shard_map/ppermute | solution.py:95
  693.2 4.7 fusion.51
  706.6 6.0 collective-permute-done.52
  715.1 5.8 collective-permute-start.53
  720.9 18.3 %collective-permute-done.46 = bf16[32,4096]{1,0:T(8,128)(2,1)S(1)} collective-permute-done((bf16[32,4096]{1,0:T(8,128)(2,1)S(1)}, bf16[32,4096]{1,0:T(8,128)(2,1)S(1)}, u32[]{:S(2)}, u32[]{:S(2)}) %collective-permute-start.46) | collective-permute-done | bytes 262176 | tf_op jit(solution)/shard_map/ppermute | solution.py:112
  740.1 8.6 %collective-permute-done.54 = bf16[128,1024]{1,0:T(8,128)(2,1)S(1)} collective-permute-done((bf16[128,1024]{1,0:T(8,128)(2,1)S(1)}, bf16[128,1024]{1,0:T(8,128)(2,1)S(1)}, u32[]{:S(2)}, u32[]{:S(2)}) %collective-permute-start.54) | collective-permute-done | bytes 262176 | tf_op jit(solution)/shard_map/ppermute | solution.py:112
  (559 shorter events, 268.8 us)
Async XLA Ops:
  5.6 20.2 %collective-permute-start.1 = (bf16[32,4224]{1,0:T(8,128)(2,1)S(1)}, bf16[32,4224]{1,0:T(8,128)(2,1)S(1)}, u32[]{:S(2)}, u32[]{:S(2)}) collective-permute-start(bf16[32,4224]{1,0:T(8,128)(2,1)S(1)} %pad_maximum_fusion.25), channel_id=1, source_target_pairs={{0,16},{1,17},{2,18},{3,19},{4,20},{5,21},{6,22},{7,23},{8,24},{9,... | collective-permute-start | bytes 811016 | tf_op jit(solution)/shard_map/ppermute | solution.py:112
  8.2 17.6 %collective-permute-start = (bf16[32,4224]{1,0:T(8,128)(2,1)S(1)}, bf16[32,4224]{1,0:T(8,128)(2,1)S(1)}, u32[]{:S(2)}, u32[]{:S(2)}) collective-permute-start(bf16[32,4224]{1,0:T(8,128)(2,1)S(1)} %pad_maximum_fusion.25), channel_id=1, source_target_pairs={{0,24},{1,25},{2,26},{3,27},{4,28},{5,29},{6,30},{7,31},{8,0},{9,1... | collective-permute-start | bytes 811016 | tf_op jit(solution)/shard_map/ppermute | solution.py:112
  33.2 23.5 %collective-permute-start.9 = (bf16[32,4096]{1,0:T(8,128)(2,1)S(1)}, bf16[32,4096]{1,0:T(8,128)(2,1)S(1)}, u32[]{:S(2)}, u32[]{:S(2)}) collective-permute-start(bf16[32,4096]{1,0:T(8,128)(2,1)S(1)} %copy-done.87), channel_id=1, source_target_pairs={{0,16},{1,17},{2,18},{3,19},{4,20},{5,21},{6,22},{7,23},{8,24},{9,... | collective-permute-start | bytes 786440 | tf_op jit(solution)/shard_map/ppermute | solution.py:112
  33.6 23.1 %collective-permute-start.10 = (bf16[32,4096]{1,0:T(8,128)(2,1)S(1)}, bf16[32,4096]{1,0:T(8,128)(2,1)S(1)}, u32[]{:S(2)}, u32[]{:S(2)}) collective-permute-start(bf16[32,4096]{1,0:T(8,128)(2,1)S(1)} %copy-done.87), channel_id=1, source_target_pairs={{0,8},{1,9},{2,10},{3,11},{4,12},{5,13},{6,14},{7,15},{8,16},{9,17... | collective-permute-start | bytes 786440 | tf_op jit(solution)/shard_map/ppermute | solution.py:112
  33.9 23.6 %collective-permute-start.5 = (bf16[128,2176]{1,0:T(8,128)(2,1)S(1)}, bf16[128,2176]{1,0:T(8,128)(2,1)S(1)}, u32[]{:S(2)}, u32[]{:S(2)}) collective-permute-start(bf16[128,2176]{1,0:T(8,128)(2,1)S(1)} %pad_maximum_fusion.19), channel_id=1, source_target_pairs={{0,2},{1,3},{2,0},{3,1},{4,6},{5,7},{6,4},{7,5},{8,10},{9,11},{10,... | collective-permute-start | bytes 1671176 | tf_op jit(solution)/shard_map/ppermute | solution.py:95
  35.5 23.6 %collective-permute-start.3 = (bf16[128,2048]{1,0:T(8,128)(2,1)S(1)}, bf16[128,2048]{1,0:T(8,128)(2,1)S(1)}, u32[]{:S(2)}, u32[]{:S(2)}) collective-permute-start(bf16[128,2048]{1,0:T(8,128)(2,1)S(1)} %pad_maximum_fusion.24), channel_id=1, source_target_pairs={{0,4},{1,5},{2,6},{3,7},{4,0},{5,1},{6,2},{7,3},{8,12},{9,13},{10,... | collective-permute-start | bytes 1572872 | tf_op jit(solution)/shard_map/ppermute | solution.py:95
  56.7 46.4 %collective-permute-start.16 = (bf16[128,1024]{1,0:T(8,128)(2,1)}, bf16[128,1024]{1,0:T(8,128)(2,1)}, u32[]{:S(2)}, u32[]{:S(2)}) collective-permute-start(bf16[128,1024]{1,0:T(8,128)(2,1)} %param.22), channel_id=1, source_target_pairs={{0,24},{1,25},{2,26},{3,27},{4,28},{5,29},{6,30},{7,31},{8,0},{9,1... | collective-permute-start | bytes 786440 | tf_op jit(solution)/shard_map/ppermute | solution.py:112
  56.7 49.0 %collective-permute-start.17 = (bf16[128,1024]{1,0:T(8,128)(2,1)}, bf16[128,1024]{1,0:T(8,128)(2,1)}, u32[]{:S(2)}, u32[]{:S(2)}) collective-permute-start(bf16[128,1024]{1,0:T(8,128)(2,1)} %param.22), channel_id=1, source_target_pairs={{0,16},{1,17},{2,18},{3,19},{4,20},{5,21},{6,22},{7,23},{8,24},{9,... | collective-permute-start | bytes 786440 | tf_op jit(solution)/shard_map/ppermute | solution.py:112
  57.6 25.5 %collective-permute-start.6 = (bf16[256,2176]{1,0:T(8,128)(2,1)S(1)}, bf16[256,2176]{1,0:T(8,128)(2,1)S(1)}, u32[]{:S(2)}, u32[]{:S(2)}) collective-permute-start(bf16[256,2176]{1,0:T(8,128)(2,1)S(1)} %pad_maximum_fusion.9), channel_id=1, source_target_pairs={{0,4},{1,5},{2,6},{3,7},{4,0},{5,1},{6,2},{7,3},{8,12},{9,13},{10,... | collective-permute-start | bytes 3342344 | tf_op jit(solution)/shard_map/ppermute | solution.py:95
  59.3 23.9 %collective-permute-start.4 = (bf16[256,2048]{1,0:T(8,128)(2,1)S(1)}, bf16[256,2048]{1,0:T(8,128)(2,1)S(1)}, u32[]{:S(2)}, u32[]{:S(2)}) collective-permute-start(bf16[256,2048]{1,0:T(8,128)(2,1)S(1)} %pad_maximum_fusion.10), channel_id=1, source_target_pairs={{0,2},{1,3},{2,0},{3,1},{4,6},{5,7},{6,4},{7,5},{8,10},{9,11},{10,... | collective-permute-start | bytes 3145736 | tf_op jit(solution)/shard_map/ppermute | solution.py:95
  98.5 112.4 %collective-permute-start.7 = (bf16[512,4224]{1,0:T(8,128)(2,1)}, bf16[512,4224]{1,0:T(8,128)(2,1)}, u32[]{:S(2)}, u32[]{:S(2)}) collective-permute-start(bf16[512,4224]{1,0:T(8,128)(2,1)} %maximum_maximum_fusion), channel_id=1, source_target_pairs={{0,1},{1,0},{2,3},{3,2},{4,5},{5,4},{6,7},{7,6},{8,9},{9,8},{10,11... | collective-permute-start | bytes 12976136 | tf_op jit(solution)/shard_map/ppermute | solution.py:95
  103.1 16.2 %collective-permute-start.11 = (bf16[128,2048]{1,0:T(8,128)(2,1)}, bf16[128,2048]{1,0:T(8,128)(2,1)S(1)}, u32[]{:S(2)}, u32[]{:S(2)}) collective-permute-start(bf16[128,2048]{1,0:T(8,128)(2,1)} %get-tuple-element.195), channel_id=1, source_target_pairs={{0,4},{1,5},{2,6},{3,7},{4,0},{5,1},{6,2},{7,3},{8,12},{9,13},{10,... | collective-permute-start | bytes 1572872 | tf_op jit(solution)/shard_map/ppermute | solution.py:95
  115.6 39.0 %collective-permute-start.14 = (bf16[256,2048]{1,0:T(8,128)(2,1)S(1)}, bf16[256,2048]{1,0:T(8,128)(2,1)S(1)}, u32[]{:S(2)}, u32[]{:S(2)}) collective-permute-start(bf16[256,2048]{1,0:T(8,128)(2,1)S(1)} %pad_maximum_fusion.12), channel_id=1, source_target_pairs={{0,4},{1,5},{2,6},{3,7},{4,0},{5,1},{6,2},{7,3},{8,12},{9,13},{10,... | collective-permute-start | bytes 3145736 | tf_op jit(solution)/shard_map/ppermute | solution.py:95
  118.8 34.1 %collective-permute-start.19 = (bf16[512,512]{1,0:T(8,128)(2,1)S(1)}, bf16[512,512]{1,0:T(8,128)(2,1)S(1)}, u32[]{:S(2)}, u32[]{:S(2)}) collective-permute-start(bf16[512,512]{1,0:T(8,128)(2,1)S(1)} %get-tuple-element.191), channel_id=1, source_target_pairs={{0,4},{1,5},{2,6},{3,7},{4,0},{5,1},{6,2},{7,3},{8,12},{9,13},{10,... | collective-permute-start | bytes 1572872 | tf_op jit(solution)/shard_map/ppermute | solution.py:95
  119.4 35.3 %collective-permute-start.12 = (bf16[256,2048]{1,0:T(8,128)(2,1)S(1)}, bf16[256,2048]{1,0:T(8,128)(2,1)S(1)}, u32[]{:S(2)}, u32[]{:S(2)}) collective-permute-start(bf16[256,2048]{1,0:T(8,128)(2,1)S(1)} %pad_maximum_fusion.11), channel_id=1, source_target_pairs={{0,2},{1,3},{2,0},{3,1},{4,6},{5,7},{6,4},{7,5},{8,10},{9,11},{10,... | collective-permute-start | bytes 3145736 | tf_op jit(solution)/shard_map/ppermute | solution.py:95
  132.2 46.9 %collective-permute-start.22 = (bf16[1024,512]{1,0:T(8,128)(2,1)S(1)}, bf16[1024,512]{1,0:T(8,128)(2,1)S(1)}, u32[]{:S(2)}, u32[]{:S(2)}) collective-permute-start(bf16[1024,512]{1,0:T(8,128)(2,1)S(1)} %pad_maximum_fusion.14), channel_id=1, source_target_pairs={{0,4},{1,5},{2,6},{3,7},{4,0},{5,1},{6,2},{7,3},{8,12},{9,13},{10,... | collective-permute-start | bytes 3145736 | tf_op jit(solution)/shard_map/ppermute | solution.py:95
  153.0 26.2 %collective-permute-start.20 = (bf16[1024,512]{1,0:T(8,128)(2,1)S(1)}, bf16[1024,512]{1,0:T(8,128)(2,1)S(1)}, u32[]{:S(2)}, u32[]{:S(2)}) collective-permute-start(bf16[1024,512]{1,0:T(8,128)(2,1)S(1)} %pad_maximum_fusion.13), channel_id=1, source_target_pairs={{0,2},{1,3},{2,0},{3,1},{4,6},{5,7},{6,4},{7,5},{8,10},{9,11},{10,... | collective-permute-start | bytes 3145736 | tf_op jit(solution)/shard_map/ppermute | solution.py:95
  179.0 64.2 %collective-permute-start.15 = (bf16[512,4096]{1,0:T(8,128)(2,1)}, bf16[512,4096]{1,0:T(8,128)(2,1)}, u32[]{:S(2)}, u32[]{:S(2)}) collective-permute-start(bf16[512,4096]{1,0:T(8,128)(2,1)} %maximum_maximum_fusion.1), channel_id=1, source_target_pairs={{0,1},{1,0},{2,3},{3,2},{4,5},{5,4},{6,7},{7,6},{8,9},{9,8},{10,11... | collective-permute-start | bytes 12582920 | tf_op jit(solution)/shard_map/ppermute | solution.py:95
  210.3 54.5 %collective-permute-start.23 = (bf16[2048,1024]{1,0:T(8,128)(2,1)}, bf16[2048,1024]{1,0:T(8,128)(2,1)}, u32[]{:S(2)}, u32[]{:S(2)}) collective-permute-start(bf16[2048,1024]{1,0:T(8,128)(2,1)} %maximum_maximum_fusion.2), channel_id=1, source_target_pairs={{0,1},{1,0},{2,3},{3,2},{4,5},{5,4},{6,7},{7,6},{8,9},{9,8},{10,11... | collective-permute-start | bytes 12582920 | tf_op jit(solution)/shard_map/ppermute | solution.py:95
  277.1 20.2 %all-to-all-start = ((bf16[8,32,1024]{2,1,0:T(8,128)(2,1)}), bf16[8,32,1024]{2,1,0:T(8,128)(2,1)S(1)}, u32[]{:S(2)}, u32[]{:S(2)}) async-start(bf16[8,32,1024]{2,1,0:T(8,128)(2,1)} %bitcast.14), calls=%async_computation | async-start | bytes 1048576 | tf_op jit(solution)/shard_map/all_to_all | solution.py:264
  297.3 18.3 %all-to-all-start.2 = ((bf16[8,32,1024]{2,1,0:T(8,128)(2,1)}), bf16[8,32,1024]{2,1,0:T(8,128)(2,1)S(1)}, u32[]{:S(2)}, u32[]{:S(2)}) async-start(bf16[8,32,1024]{2,1,0:T(8,128)(2,1)} %bitcast.327), calls=%async_computation.2 | async-start | bytes 1048576 | tf_op jit(solution)/shard_map/all_to_all | solution.py:264
  343.1 40.2 %all-to-all-start.3 = ((bf16[8,32,1024]{2,1,0:T(8,128)(2,1)}), bf16[8,32,1024]{2,1,0:T(8,128)(2,1)}, u32[]{:S(2)}, u32[]{:S(2)}) async-start(bf16[8,32,1024]{2,1,0:T(8,128)(2,1)} %bitcast.326), calls=%async_computation.3 | async-start | bytes 1048576 | tf_op jit(solution)/shard_map/all_to_all | solution.py:273
  363.2 168.2 %collective-permute-start.56 = (bf16[512,4224]{1,0:T(8,128)(2,1)}, bf16[512,4224]{1,0:T(8,128)(2,1)}, u32[]{:S(2)}, u32[]{:S(2)}) collective-permute-start(bf16[512,4224]{1,0:T(8,128)(2,1)} %pad_maximum_fusion.3), channel_id=1, source_target_pairs={{0,1},{1,0},{2,3},{3,2},{4,5},{5,4},{6,7},{7,6},{8,9},{9,8},{10,11... | collective-permute-start | bytes 12976136 | tf_op jit(solution)/shard_map/ppermute | solution.py:95
  377.5 145.2 %collective-permute-start.58 = (bf16[2048,1024]{1,0:T(8,128)(2,1)}, bf16[2048,1024]{1,0:T(8,128)(2,1)}, u32[]{:S(2)}, u32[]{:S(2)}) collective-permute-start(bf16[2048,1024]{1,0:T(8,128)(2,1)} %convolution_convert_fusion.3), channel_id=1, source_target_pairs={{0,1},{1,0},{2,3},{3,2},{4,5},{5,4},{6,7},{7,6},{8,9},{9,8},{10,11... | collective-permute-start | bytes 12582920 | tf_op jit(solution)/shard_map/ppermute | solution.py:95
  383.3 118.5 %all-to-all-start.1 = ((bf16[8,32,1024]{2,1,0:T(8,128)(2,1)}), bf16[8,32,1024]{2,1,0:T(8,128)(2,1)}, u32[]{:S(2)}, u32[]{:S(2)}) async-start(bf16[8,32,1024]{2,1,0:T(8,128)(2,1)} %bitcast.21), calls=%async_computation.1 | async-start | bytes 1048576 | tf_op jit(solution)/shard_map/all_to_all | solution.py:273
  472.6 40.0 %collective-permute-start.24 = (bf16[512,3200]{1,0:T(8,128)(2,1)}, bf16[512,3200]{1,0:T(8,128)(2,1)}, u32[]{:S(2)}, u32[]{:S(2)}) collective-permute-start(bf16[512,3200]{1,0:T(8,128)(2,1)} %pad_maximum_fusion.4), channel_id=1, source_target_pairs={{0,1},{1,0},{2,3},{3,2},{4,5},{5,4},{6,7},{7,6},{8,9},{9,8},{10,11... | collective-permute-start | bytes 9830408 | tf_op jit(solution)/shard_map/ppermute | solution.py:95
  509.5 41.7 %collective-permute-start.40 = (bf16[512,4096]{1,0:T(8,128)(2,1)}, bf16[512,4096]{1,0:T(8,128)(2,1)}, u32[]{:S(2)}, u32[]{:S(2)}) collective-permute-start(bf16[512,4096]{1,0:T(8,128)(2,1)} %convolution_convert_fusion.1), channel_id=1, source_target_pairs={{0,1},{1,0},{2,3},{3,2},{4,5},{5,4},{6,7},{7,6},{8,9},{9,8},{10,11... | collective-permute-start | bytes 12582920 | tf_op jit(solution)/shard_map/ppermute | solution.py:95
  511.0 47.9 %collective-permute-start.48 = (bf16[2048,1024]{1,0:T(8,128)(2,1)}, bf16[2048,1024]{1,0:T(8,128)(2,1)}, u32[]{:S(2)}, u32[]{:S(2)}) collective-permute-start(bf16[2048,1024]{1,0:T(8,128)(2,1)} %convolution_convert_fusion.4), channel_id=1, source_target_pairs={{0,1},{1,0},{2,3},{3,2},{4,5},{5,4},{6,7},{7,6},{8,9},{9,8},{10,11... | collective-permute-start | bytes 12582920 | tf_op jit(solution)/shard_map/ppermute | solution.py:95
  522.1 26.6 %collective-permute-start.27 = (bf16[256,1664]{1,0:T(8,128)(2,1)}, bf16[256,1664]{1,0:T(8,128)(2,1)}, u32[]{:S(2)}, u32[]{:S(2)}) collective-permute-start(bf16[256,1664]{1,0:T(8,128)(2,1)} %pad_maximum_fusion.17), channel_id=1, source_target_pairs={{0,4},{1,5},{2,6},{3,7},{4,0},{5,1},{6,2},{7,3},{8,12},{9,13},{10,... | collective-permute-start | bytes 2555912 | tf_op jit(solution)/shard_map/ppermute | solution.py:95
  522.7 22.5 %collective-permute-start.25 = (bf16[256,1536]{1,0:T(8,128)(2,1)}, bf16[256,1536]{1,0:T(8,128)(2,1)}, u32[]{:S(2)}, u32[]{:S(2)}) collective-permute-start(bf16[256,1536]{1,0:T(8,128)(2,1)} %slice.511), channel_id=1, source_target_pairs={{0,2},{1,3},{2,0},{3,1},{4,6},{5,7},{6,4},{7,5},{8,10},{9,11},{10,... | collective-permute-start | bytes 2359304 | tf_op jit(solution)/shard_map/ppermute | solution.py:95
  531.3 160.3 %collective-permute-start.59 = (bf16[1024,1024]{1,0:T(8,128)(2,1)}, bf16[1024,1024]{1,0:T(8,128)(2,1)}, u32[]{:S(2)}, u32[]{:S(2)}) collective-permute-start(bf16[1024,1024]{1,0:T(8,128)(2,1)} %slice.726), channel_id=1, source_target_pairs={{0,2},{1,3},{2,0},{3,1},{4,6},{5,7},{6,4},{7,5},{8,10},{9,11},{10,... | collective-permute-start | bytes 6291464 | tf_op jit(solution)/shard_map/ppermute | solution.py:95
  547.2 15.6 %collective-permute-start.26 = (bf16[128,1536]{1,0:T(8,128)(2,1)S(1)}, bf16[128,1536]{1,0:T(8,128)(2,1)S(1)}, u32[]{:S(2)}, u32[]{:S(2)}) collective-permute-start(bf16[128,1536]{1,0:T(8,128)(2,1)S(1)} %slice.732), channel_id=1, source_target_pairs={{0,4},{1,5},{2,6},{3,7},{4,0},{5,1},{6,2},{7,3},{8,12},{9,13},{10,... | collective-permute-start | bytes 1179656 | tf_op jit(solution)/shard_map/ppermute | solution.py:95
  550.1 47.2 %collective-permute-start.28 = (bf16[128,1664]{1,0:T(8,128)(2,1)S(1)}, bf16[128,1664]{1,0:T(8,128)(2,1)S(1)}, u32[]{:S(2)}, u32[]{:S(2)}) collective-permute-start(bf16[128,1664]{1,0:T(8,128)(2,1)S(1)} %slice.731), channel_id=1, source_target_pairs={{0,2},{1,3},{2,0},{3,1},{4,6},{5,7},{6,4},{7,5},{8,10},{9,11},{10,... | collective-permute-start | bytes 1277960 | tf_op jit(solution)/shard_map/ppermute | solution.py:95
  555.8 64.1 %collective-permute-start.41 = (bf16[256,2048]{1,0:T(8,128)(2,1)}, bf16[256,2048]{1,0:T(8,128)(2,1)}, u32[]{:S(2)}, u32[]{:S(2)}) collective-permute-start(bf16[256,2048]{1,0:T(8,128)(2,1)} %slice.546), channel_id=1, source_target_pairs={{0,2},{1,3},{2,0},{3,1},{4,6},{5,7},{6,4},{7,5},{8,10},{9,11},{10,... | collective-permute-start | bytes 3145736 | tf_op jit(solution)/shard_map/ppermute | solution.py:95
  599.7 15.6 %collective-permute-start.30 = (bf16[32,3200]{1,0:T(8,128)(2,1)S(1)}, bf16[32,3200]{1,0:T(8,128)(2,1)S(1)}, u32[]{:S(2)}, u32[]{:S(2)}) collective-permute-start(bf16[32,3200]{1,0:T(8,128)(2,1)S(1)} %get-tuple-element.201), channel_id=1, source_target_pairs={{0,16},{1,17},{2,18},{3,19},{4,20},{5,21},{6,22},{7,23},{8,24},{9,... | collective-permute-start | bytes 614408 | tf_op jit(solution)/shard_map/ppermute | solution.py:112
  599.7 17.1 %collective-permute-start.29 = (bf16[32,3200]{1,0:T(8,128)(2,1)S(1)}, bf16[32,3200]{1,0:T(8,128)(2,1)S(1)}, u32[]{:S(2)}, u32[]{:S(2)}) collective-permute-start(bf16[32,3200]{1,0:T(8,128)(2,1)S(1)} %get-tuple-element.199), channel_id=1, source_target_pairs={{0,8},{1,9},{2,10},{3,11},{4,12},{5,13},{6,14},{7,15},{8,16},{9,17... | collective-permute-start | bytes 614408 | tf_op jit(solution)/shard_map/ppermute | solution.py:112
  605.2 92.6 %collective-permute-start.57 = (bf16[256,4224]{1,0:T(8,128)(2,1)S(1)}, bf16[256,4224]{1,0:T(8,128)(2,1)}, u32[]{:S(2)}, u32[]{:S(2)}) collective-permute-start(bf16[256,4224]{1,0:T(8,128)(2,1)S(1)} %copy-done.66), channel_id=1, source_target_pairs={{0,2},{1,3},{2,0},{3,1},{4,6},{5,7},{6,4},{7,5},{8,10},{9,11},{10,... | collective-permute-start | bytes 6488072 | tf_op jit(solution)/shard_map/ppermute | solution.py:95
  615.3 26.1 %collective-permute-start.43 = (bf16[256,2048]{1,0:T(8,128)(2,1)S(1)}, bf16[256,2048]{1,0:T(8,128)(2,1)S(1)}, u32[]{:S(2)}, u32[]{:S(2)}) collective-permute-start(bf16[256,2048]{1,0:T(8,128)(2,1)S(1)} %pad_maximum_fusion.15), channel_id=1, source_target_pairs={{0,4},{1,5},{2,6},{3,7},{4,0},{5,1},{6,2},{7,3},{8,12},{9,13},{10,... | collective-permute-start | bytes 3145736 | tf_op jit(solution)/shard_map/ppermute | solution.py:95
  616.8 71.2 %collective-permute-start.49 = (bf16[1024,512]{1,0:T(8,128)(2,1)S(1)}, bf16[1024,512]{1,0:T(8,128)(2,1)S(1)}, u32[]{:S(2)}, u32[]{:S(2)}) collective-permute-start(bf16[1024,512]{1,0:T(8,128)(2,1)S(1)} %slice.563), channel_id=1, source_target_pairs={{0,2},{1,3},{2,0},{3,1},{4,6},{5,7},{6,4},{7,5},{8,10},{9,11},{10,... | collective-permute-start | bytes 3145736 | tf_op jit(solution)/shard_map/ppermute | solution.py:95
  619.9 69.6 %collective-permute-start.51 = (bf16[1024,512]{1,0:T(8,128)(2,1)S(1)}, bf16[1024,512]{1,0:T(8,128)(2,1)S(1)}, u32[]{:S(2)}, u32[]{:S(2)}) collective-permute-start(bf16[1024,512]{1,0:T(8,128)(2,1)S(1)} %pad_maximum_fusion.16), channel_id=1, source_target_pairs={{0,4},{1,5},{2,6},{3,7},{4,0},{5,1},{6,2},{7,3},{8,12},{9,13},{10,... | collective-permute-start | bytes 3145736 | tf_op jit(solution)/shard_map/ppermute | solution.py:95
  641.4 61.9 %collective-permute-start.42 = (bf16[128,2048]{1,0:T(8,128)(2,1)}, bf16[128,2048]{1,0:T(8,128)(2,1)S(1)}, u32[]{:S(2)}, u32[]{:S(2)}) collective-permute-start(bf16[128,2048]{1,0:T(8,128)(2,1)} %slice.730), channel_id=1, source_target_pairs={{0,4},{1,5},{2,6},{3,7},{4,0},{5,1},{6,2},{7,3},{8,12},{9,13},{10,... | collective-permute-start | bytes 1572872 | tf_op jit(solution)/shard_map/ppermute | solution.py:95
  689.5 16.9 %collective-permute-start.50 = (bf16[512,512]{1,0:T(8,128)(2,1)S(1)}, bf16[512,512]{1,0:T(8,128)(2,1)S(1)}, u32[]{:S(2)}, u32[]{:S(2)}) collective-permute-start(bf16[512,512]{1,0:T(8,128)(2,1)S(1)} %slice.728), channel_id=1, source_target_pairs={{0,4},{1,5},{2,6},{3,7},{4,0},{5,1},{6,2},{7,3},{8,12},{9,13},{10,... | collective-permute-start | bytes 1572872 | tf_op jit(solution)/shard_map/ppermute | solution.py:95
  691.6 21.0 %collective-permute-start.52 = (bf16[512,512]{1,0:T(8,128)(2,1)}, bf16[512,512]{1,0:T(8,128)(2,1)S(1)}, u32[]{:S(2)}, u32[]{:S(2)}) collective-permute-start(bf16[512,512]{1,0:T(8,128)(2,1)} %slice.727), channel_id=1, source_target_pairs={{0,2},{1,3},{2,0},{3,1},{4,6},{5,7},{6,4},{7,5},{8,10},{9,11},{10,... | collective-permute-start | bytes 1572872 | tf_op jit(solution)/shard_map/ppermute | solution.py:95
  705.8 33.4 %collective-permute-start.46 = (bf16[32,4096]{1,0:T(8,128)(2,1)S(1)}, bf16[32,4096]{1,0:T(8,128)(2,1)S(1)}, u32[]{:S(2)}, u32[]{:S(2)}) collective-permute-start(bf16[32,4096]{1,0:T(8,128)(2,1)S(1)} %get-tuple-element.188), channel_id=1, source_target_pairs={{0,16},{1,17},{2,18},{3,19},{4,20},{5,21},{6,22},{7,23},{8,24},{9,... | collective-permute-start | bytes 786440 | tf_op jit(solution)/shard_map/ppermute | solution.py:112
  705.8 33.4 %collective-permute-start.45 = (bf16[32,4096]{1,0:T(8,128)(2,1)S(1)}, bf16[32,4096]{1,0:T(8,128)(2,1)S(1)}, u32[]{:S(2)}, u32[]{:S(2)}) collective-permute-start(bf16[32,4096]{1,0:T(8,128)(2,1)S(1)} %get-tuple-element.186), channel_id=1, source_target_pairs={{0,8},{1,9},{2,10},{3,11},{4,12},{5,13},{6,14},{7,15},{8,16},{9,17... | collective-permute-start | bytes 786440 | tf_op jit(solution)/shard_map/ppermute | solution.py:112
  713.0 27.1 %collective-permute-start.55 = (bf16[128,1024]{1,0:T(8,128)(2,1)S(1)}, bf16[128,1024]{1,0:T(8,128)(2,1)S(1)}, u32[]{:S(2)}, u32[]{:S(2)}) collective-permute-start(bf16[128,1024]{1,0:T(8,128)(2,1)S(1)} %get-tuple-element.184), channel_id=1, source_target_pairs={{0,24},{1,25},{2,26},{3,27},{4,28},{5,29},{6,30},{7,31},{8,0},{9,1... | collective-permute-start | bytes 786440 | tf_op jit(solution)/shard_map/ppermute | solution.py:112
  715.1 33.6 %collective-permute-start.54 = (bf16[128,1024]{1,0:T(8,128)(2,1)S(1)}, bf16[128,1024]{1,0:T(8,128)(2,1)S(1)}, u32[]{:S(2)}, u32[]{:S(2)}) collective-permute-start(bf16[128,1024]{1,0:T(8,128)(2,1)S(1)} %get-tuple-element.185), channel_id=1, source_target_pairs={{0,16},{1,17},{2,18},{3,19},{4,20},{5,21},{6,22},{7,23},{8,24},{9,... | collective-permute-start | bytes 786440 | tf_op jit(solution)/shard_map/ppermute | solution.py:112
  715.1 33.6 %collective-permute-start.53 = (bf16[128,1024]{1,0:T(8,128)(2,1)S(1)}, bf16[128,1024]{1,0:T(8,128)(2,1)S(1)}, u32[]{:S(2)}, u32[]{:S(2)}) collective-permute-start(bf16[128,1024]{1,0:T(8,128)(2,1)S(1)} %get-tuple-element.183), channel_id=1, source_target_pairs={{0,8},{1,9},{2,10},{3,11},{4,12},{5,13},{6,14},{7,15},{8,16},{9,17... | collective-permute-start | bytes 786440 | tf_op jit(solution)/shard_map/ppermute | solution.py:112
  (112 other events, 1548.7 us)
